TPU v7x, 32 devices: a whole 2x2x4 slice. The times are simulated.
32 devices in a mesh: section: 8 (over z, core), dp: 4 (over y, x).
Axes of the slice: x: 2, y: 2, z: 4, core: 2. Of those that a mesh axis runs over, the one named last changes fastest.
Arguments:
- stream_in: bfloat16 [8, 2, 256, 6144], P('section', None, 'dp'), may hold values from -600 to 600
- gain: bfloat16 [8, 6144], P('section'), may hold values from 0.5 to 1.5
- kv_weight: bfloat16 [8, 6144, 1024], P('section'), may hold values from -21 to 21
- pattern: int32 [2, 2, 2], replicated, may hold values from 0 to 1, as said below
- top_grad: bfloat16 [2, 256, 6144], P(None, 'dp'), may hold values from -6 to 6
Outputs:
- stream_grads: bfloat16 [8, 2, 256, 6144], P('section', None, 'dp')
- weight_grads: bfloat16 [8, 6144, 1024], P('section', 'dp')
Inputs may be any that keep to these rules, and one draw needn't show every extreme that they name: `pattern`: entries are 0 or 1; tiles above the diagonal are 0 and diagonal tiles are 1.
All inputs are finite; a program needn't handle non-finite values.
Results may differ from a plain program's by a relative error of at most 0.03.
The roundings to bfloat16 on the way count: a program that leaves them out, or rounds other values in their place, can miss the bound.
Values may be sent and summed in bfloat16 or wider, within the bound.
A program may use at most 128 MiB of HBM per device.

v0:
```python
import math

import jax
import jax.numpy as jnp
from jax import lax
from jax.sharding import PartitionSpec as P

H = 48
DH = 128
KVH = 4
TILE = 128


def from_behind(x, axis, by):
    devices = lax.axis_size(axis)
    pairs = [(i, i + by) for i in range(devices) if 0 <= i + by < devices]
    return lax.ppermute(x, axis, pairs)


def shards(stream_in, gain, kv_weight, pattern, top_grad):
    section_count = lax.axis_size("section")
    my_section = lax.axis_index("section")
    my_rank = lax.axis_index("dp")
    rank_count = lax.axis_size("dp")
    micro_count = stream_in.shape[1]
    tokens = stream_in.shape[2]
    model_width = stream_in.shape[3]
    weight_matrix = kv_weight[0]
    kv_width = weight_matrix.shape[1] // 2
    head_size = DH
    group_size = H // KVH
    seq_length = tokens * rank_count
    tile_total_count = seq_length // TILE
    score_scale = 1.0 / math.sqrt(head_size)
    gain_f = gain[0].astype(jnp.float32)
    local_stream = stream_in[0]
    query_pos = my_rank * tokens + jnp.arange(tokens)
    key_pos = jnp.arange(seq_length)
    causal = key_pos[None, :] <= query_pos[:, None]
    row_pick = (query_pos[:, None] // TILE == jnp.arange(tile_total_count)[None, :]).astype(
        jnp.float32
    )
    col_pick = (jnp.arange(tile_total_count)[:, None] == key_pos[None, :] // TILE).astype(
        jnp.float32
    )
    tile_hits = jnp.einsum("qa,mab,bk->mqk", row_pick, pattern.astype(jnp.float32), col_pick)
    allowed_all = (tile_hits > 0.5) & causal[None]

    def norm_stats(slot):
        stream = lax.dynamic_index_in_dim(local_stream, slot, 0, keepdims=False)
        stream_f = stream.astype(jnp.float32)
        inverse_rms = lax.rsqrt(jnp.mean(stream_f * stream_f, axis=-1, keepdims=True) + 1e-05)
        return (stream_f, inverse_rms)

    def project_pass(slot):
        stream_f, inverse_rms = norm_stats(slot)
        normalized_rows = (stream_f * inverse_rms * gain_f).astype(jnp.bfloat16)
        keyval = jnp.dot(normalized_rows, weight_matrix, preferred_element_type=jnp.float32).astype(
            jnp.bfloat16
        )
        return (normalized_rows, keyval)

    def project_skip(slot):
        return (
            jnp.zeros((tokens, model_width), jnp.bfloat16),
            jnp.zeros((tokens, 2 * kv_width), jnp.bfloat16),
        )

    def attend_pass(operands):
        normalized_rows, keyval_all, grad_up, slot = operands
        allowed = lax.dynamic_index_in_dim(allowed_all, slot, 0, keepdims=False)
        query_parts = []
        key_parts = []
        value_parts = []
        for head_group in range(KVH):
            low = head_group * group_size * head_size
            high = low + group_size * head_size
            queries = normalized_rows[:, low:high].reshape(tokens, group_size, head_size)
            key_rows = keyval_all[:, head_group * head_size : (head_group + 1) * head_size]
            value_rows = keyval_all[
                :, kv_width + head_group * head_size : kv_width + (head_group + 1) * head_size
            ]
            scores = (
                jnp.einsum("qhd,kd->hqk", queries, key_rows, preferred_element_type=jnp.float32)
                * score_scale
            )
            scores = jnp.where(allowed[None], scores, -1e30)
            row_peak = jnp.max(scores, axis=-1, keepdims=True)
            expo = jnp.exp(scores - row_peak)
            soft_weights = expo / jnp.sum(expo, axis=-1, keepdims=True)
            soft_rounded = soft_weights.astype(jnp.bfloat16)
            attn_out = jnp.einsum(
                "hqk,kd->qhd", soft_rounded, value_rows, preferred_element_type=jnp.float32
            ).astype(jnp.bfloat16)
            heads_up = grad_up[:, low:high].reshape(tokens, group_size, head_size)
            delta = jnp.sum(heads_up.astype(jnp.float32) * attn_out.astype(jnp.float32), axis=-1)
            value_parts.append(
                jnp.einsum(
                    "hqk,qhd->kd", soft_rounded, heads_up, preferred_element_type=jnp.float32
                )
            )
            dprobs = jnp.einsum(
                "qhd,kd->hqk", heads_up, value_rows, preferred_element_type=jnp.float32
            )
            dscores = (soft_weights * (dprobs - delta.T[:, :, None]) * score_scale).astype(
                jnp.bfloat16
            )
            query_parts.append(
                jnp.einsum(
                    "hqk,kd->qhd", dscores, key_rows, preferred_element_type=jnp.float32
                ).reshape(tokens, group_size * head_size)
            )
            key_parts.append(
                jnp.einsum("hqk,qhd->kd", dscores, queries, preferred_element_type=jnp.float32)
            )
        return (
            jnp.concatenate(key_parts + value_parts, axis=1),
            jnp.concatenate(query_parts, axis=1),
        )

    def attend_skip(operands):
        return (
            jnp.zeros((seq_length, 2 * kv_width), jnp.float32),
            jnp.zeros((tokens, model_width), jnp.float32),
        )

    def input_pass(operands):
        dkeyval, query_grad, grad_up, slot = operands
        stream_f, inverse_rms = norm_stats(slot)
        back_proj = lax.dot_general(
            dkeyval, weight_matrix, (((1,), (1,)), ((), ())), preferred_element_type=jnp.float32
        )
        scaled = gain_f * (query_grad + back_proj)
        grad_in = (
            grad_up.astype(jnp.float32)
            + inverse_rms * scaled
            - stream_f * inverse_rms**3 * jnp.mean(stream_f * scaled, axis=-1, keepdims=True)
        )
        return grad_in.astype(jnp.bfloat16)

    def input_skip(operands):
        return jnp.zeros((tokens, model_width), jnp.bfloat16)

    def advance(turn, state_carry):
        incoming, grads_store, normed_store, dkv_store = state_carry
        position = turn - (section_count - 1 - my_section)
        active = (position >= 0) & (position < micro_count)
        slot = jnp.clip(position, 0, micro_count - 1)
        top_slot = lax.dynamic_index_in_dim(top_grad, slot, 0, keepdims=False)
        grad_up = jnp.where(my_section == section_count - 1, top_slot, incoming)
        normalized_rows, keyval = lax.cond(active, project_pass, project_skip, slot)
        keyval_all = lax.all_gather(keyval, "dp", axis=0, tiled=True)
        partial_terms, query_grad = lax.cond(
            active, attend_pass, attend_skip, (normalized_rows, keyval_all, grad_up, slot)
        )
        dkeyval = lax.psum_scatter(
            partial_terms.astype(jnp.bfloat16), "dp", scatter_dimension=0, tiled=True
        )
        grad_in = lax.cond(active, input_pass, input_skip, (dkeyval, query_grad, grad_up, slot))

        def store_at(store, fresh):
            return jnp.where(active, lax.dynamic_update_index_in_dim(store, fresh, slot, 0), store)

        arriving = from_behind(grad_in, "section", -1)
        return (
            arriving,
            store_at(grads_store, grad_in),
            store_at(normed_store, normalized_rows),
            store_at(dkv_store, dkeyval),
        )

    initial = (
        jnp.zeros((tokens, model_width), jnp.bfloat16),
        jnp.zeros((micro_count, tokens, model_width), jnp.bfloat16),
        jnp.zeros((micro_count, tokens, model_width), jnp.bfloat16),
        jnp.zeros((micro_count, tokens, 2 * kv_width), jnp.bfloat16),
    )
    finished = lax.fori_loop(0, section_count + micro_count - 1, advance, initial)
    per_section_gradient = finished[1]
    normed_all = finished[2]
    dkv_all = finished[3]
    partial_grad = jnp.einsum(
        "mtc,mte->ce", normed_all, dkv_all, preferred_element_type=jnp.float32
    )
    owned = lax.psum_scatter(partial_grad, "dp", scatter_dimension=0, tiled=True)
    return (per_section_gradient[None], owned.astype(jnp.bfloat16)[None])


def solution(mesh):
    placed = (
        P("section", None, "dp", None),
        P("section", None),
        P("section", None, None),
        P(),
        P(None, "dp", None),
    )
    return jax.shard_map(
        shards,
        mesh=mesh,
        in_specs=placed,
        out_specs=(P("section", None, "dp", None), P("section", "dp", None)),
        check_vma=False,
    )
```

profile of v0, /device:TPU:0, one launch (start us, length us, event | category | flops | bytes accessed | tf_op | source)
XLA Modules:
  0.0 1316.8 jit_solution(14604458691813959011)
XLA Ops:
  14.9 1057.6 %while.21 = (s32[]{:T(128)}, bf16[64,6144]{1,0:T(8,128)(2,1)}, bf16[2,64,6144]{2,1,0:T(8,128)(2,1)}, bf16[2,64,6144]{2,1,0:T(8,128)(2,1)}, bf16[2,64,1024]{2,1,0...) while((s32[]{:T(128)}, bf16[64,6144]{1,0:T(8,128)(2,1)}, ...), condition=%wide.region_23.24_spmd, body=%wide.region_0.23_spmd.sunk | while | flops 3249281280 | bytes 97323576 | solution.py:178
  15.8 11.5 all_gather.10
  35.5 75.7 %reduce-scatter.5.cloned.1.call-done = bf16[64,1024]{1,0:T(8,128)(2,1)} async-done(((bf16[256,1024]{1,0:T(8,128)(2,1)}), bf16[64,1024]{1,0:T(8,128)(2,1)}) %reduce-scatter.5.cloned.1.call-update) | async-done | bytes 131088 | tf_op jit(solution)/shard_map/while/body/eval_jaxpr/reduce_scatter | solution.py:156
  118.5 10.0 all_gather.10
  136.6 87.9 %reduce-scatter.5.cloned.1.call-done = bf16[64,1024]{1,0:T(8,128)(2,1)} async-done(((bf16[256,1024]{1,0:T(8,128)(2,1)}), bf16[64,1024]{1,0:T(8,128)(2,1)}) %reduce-scatter.5.cloned.1.call-update) | async-done | bytes 131088 | tf_op jit(solution)/shard_map/while/body/eval_jaxpr/reduce_scatter | solution.py:156
  231.8 10.0 all_gather.10
  249.9 96.1 %reduce-scatter.5.cloned.1.call-done = bf16[64,1024]{1,0:T(8,128)(2,1)} async-done(((bf16[256,1024]{1,0:T(8,128)(2,1)}), bf16[64,1024]{1,0:T(8,128)(2,1)}) %reduce-scatter.5.cloned.1.call-update) | async-done | bytes 131088 | tf_op jit(solution)/shard_map/while/body/eval_jaxpr/reduce_scatter | solution.py:156
  353.4 10.0 all_gather.10
  371.5 94.5 %reduce-scatter.5.cloned.1.call-done = bf16[64,1024]{1,0:T(8,128)(2,1)} async-done(((bf16[256,1024]{1,0:T(8,128)(2,1)}), bf16[64,1024]{1,0:T(8,128)(2,1)}) %reduce-scatter.5.cloned.1.call-update) | async-done | bytes 131088 | tf_op jit(solution)/shard_map/while/body/eval_jaxpr/reduce_scatter | solution.py:156
  473.3 10.0 all_gather.10
  491.4 95.2 %reduce-scatter.5.cloned.1.call-done = bf16[64,1024]{1,0:T(8,128)(2,1)} async-done(((bf16[256,1024]{1,0:T(8,128)(2,1)}), bf16[64,1024]{1,0:T(8,128)(2,1)}) %reduce-scatter.5.cloned.1.call-update) | async-done | bytes 131088 | tf_op jit(solution)/shard_map/while/body/eval_jaxpr/reduce_scatter | solution.py:156
  594.0 9.9 all_gather.10
  612.0 93.6 %reduce-scatter.5.cloned.1.call-done = bf16[64,1024]{1,0:T(8,128)(2,1)} async-done(((bf16[256,1024]{1,0:T(8,128)(2,1)}), bf16[64,1024]{1,0:T(8,128)(2,1)}) %reduce-scatter.5.cloned.1.call-update) | async-done | bytes 131088 | tf_op jit(solution)/shard_map/while/body/eval_jaxpr/reduce_scatter | solution.py:156
  713.0 10.0 all_gather.10
  731.0 94.2 %reduce-scatter.5.cloned.1.call-done = bf16[64,1024]{1,0:T(8,128)(2,1)} async-done(((bf16[256,1024]{1,0:T(8,128)(2,1)}), bf16[64,1024]{1,0:T(8,128)(2,1)}) %reduce-scatter.5.cloned.1.call-update) | async-done | bytes 131088 | tf_op jit(solution)/shard_map/while/body/eval_jaxpr/reduce_scatter | solution.py:156
  830.0 10.6 collective-permute-done
  841.5 9.3 conditional.6
  843.7 7.1 convolution_convert_fusion
  850.8 10.0 all_gather.10
  862.2 49.5 %conditional.7 = (bf16[256,1024]{0,1:T(8,128)(2,1)}, f32[64,6144]{1,0:T(8,128)}) conditional(s32[]{:T(128)} %convert_element_type.238, () %tuple.91, (s32[]{:T(128)}, pred[2,64,256]{2,1,0:T(8,128)(4,1)S(1)}, bf16[256,1024]{1,0:T(8,128)(2,1)S(1)}, bf16[64,6144]{1,0:T(8,128)(2,1)}, bf16[64,6144]{1,0:T(8,128)(2,1)S(1)}) %tuple.94), branch_computations={%region_4.4_spmd, %region_5.17_spmd} | conditional | flops 1628706816 | bytes 38942056 | solution.py:153
  872.9 2.6 fusion.52
  880.4 2.5 fusion.53
  886.6 2.8 fusion.290
  889.4 3.2 fusion.54
  895.9 3.3 fusion.58
  899.2 3.3 fusion.57
  902.5 3.3 fusion.56
  905.8 3.3 fusion.55
  916.2 27.1 %reduce-scatter.5.cloned.1.call-done = bf16[64,1024]{1,0:T(8,128)(2,1)} async-done(((bf16[256,1024]{1,0:T(8,128)(2,1)}), bf16[64,1024]{1,0:T(8,128)(2,1)}) %reduce-scatter.5.cloned.1.call-update) | async-done | bytes 131088 | tf_op jit(solution)/shard_map/while/body/eval_jaxpr/reduce_scatter | solution.py:156
  943.3 11.6 conditional.8
  943.3 9.1 fusion.256
  960.3 9.3 conditional.6
  962.5 7.1 convolution_convert_fusion
  969.6 10.6 all_gather.10
  981.7 49.5 %conditional.7 = (bf16[256,1024]{0,1:T(8,128)(2,1)}, f32[64,6144]{1,0:T(8,128)}) conditional(s32[]{:T(128)} %convert_element_type.238, () %tuple.91, (s32[]{:T(128)}, pred[2,64,256]{2,1,0:T(8,128)(4,1)S(1)}, bf16[256,1024]{1,0:T(8,128)(2,1)S(1)}, bf16[64,6144]{1,0:T(8,128)(2,1)}, bf16[64,6144]{1,0:T(8,128)(2,1)S(1)}) %tuple.94), branch_computations={%region_4.4_spmd, %region_5.17_spmd} | conditional | flops 1628706816 | bytes 38942056 | solution.py:153
  992.4 2.6 fusion.52
  1006.1 2.8 fusion.290
  1008.9 3.2 fusion.54
  1015.4 3.3 fusion.58
  1018.7 3.3 fusion.57
  1022.0 3.3 fusion.56
  1025.3 3.3 fusion.55
  1035.7 19.7 %reduce-scatter.5.cloned.1.call-done = bf16[64,1024]{1,0:T(8,128)(2,1)} async-done(((bf16[256,1024]{1,0:T(8,128)(2,1)}), bf16[64,1024]{1,0:T(8,128)(2,1)}) %reduce-scatter.5.cloned.1.call-update) | async-done | bytes 131088 | tf_op jit(solution)/shard_map/while/body/eval_jaxpr/reduce_scatter | solution.py:156
  1055.4 11.6 conditional.8
  1055.4 9.1 fusion.256
  1072.4 13.2 %convolution_bitcast_fusion.16 = f32[6144,1024]{1,0:T(8,128)} fusion(bf16[2,64,6144]{2,1,0:T(8,128)(2,1)} %get-tuple-element.327, bf16[2,64,1024]{2,1,0:T(8,128)(2,1)} %get-tuple-element.328), kind=kOutput, calls=%fused_computation.212 | convolution fusion | flops 1610612736 | bytes 27000832 | tf_op jit(solution)/shard_map/mtc,mte->ce/dot_general | solution.py:182
  1085.6 219.1 %reduce-scatter.3.cloned.1.call-done = f32[1536,1024]{1,0:T(8,128)} async-done(((f32[6144,1024]{1,0:T(8,128)}), f32[1536,1024]{1,0:T(8,128)}) %reduce-scatter.3.cloned.1.call-update) | async-done | bytes 6291472 | tf_op jit(solution)/shard_map/reduce_scatter | solution.py:185
  1304.7 4.9 convert_bitcast_fusion
  (367 shorter events, 226.9 us)
Async XLA Ops:
  14.9 13.9 %copy-start.13 = (pred[2,64,256]{2,1,0:T(8,128)(4,1)}, pred[2,64,256]{2,1,0:T(8,128)(4,1)S(1)}, u32[]{:S(2)}) copy-start(pred[2,64,256]{2,1,0:T(8,128)(4,1)S(1)} %get-tuple-element.519) | copy-start | bytes 98308 | tf_op jit(solution)/shard_map/while
  14.9 96.3 %reduce-scatter.5.cloned.1.call-start = ((), (), s32[]{:S(2)}) async-start(), calls=%async_computation.3 | async-start | bytes 655360 | tf_op jit(solution)/shard_map/while/body/eval_jaxpr/reduce_scatter | solution.py:156
  112.1 3.6 copy-start.8
  112.1 5.4 copy-start.14
  112.1 4.5 collective-permute-start
  117.5 12.4 copy-start.13
  117.5 106.9 %reduce-scatter.5.cloned.1.call-start = ((), (), s32[]{:S(2)}) async-start(), calls=%async_computation.3 | async-start | bytes 655360 | tf_op jit(solution)/shard_map/while/body/eval_jaxpr/reduce_scatter | solution.py:156
  225.5 3.6 copy-start.8
  225.5 5.4 copy-start.14
  225.5 4.5 collective-permute-start
  230.9 12.4 copy-start.13
  230.9 115.1 %reduce-scatter.5.cloned.1.call-start = ((), (), s32[]{:S(2)}) async-start(), calls=%async_computation.3 | async-start | bytes 655360 | tf_op jit(solution)/shard_map/while/body/eval_jaxpr/reduce_scatter | solution.py:156
  347.0 3.6 copy-start.8
  347.0 5.4 copy-start.14
  347.0 4.5 collective-permute-start
  352.4 12.4 copy-start.13
  352.4 113.5 %reduce-scatter.5.cloned.1.call-start = ((), (), s32[]{:S(2)}) async-start(), calls=%async_computation.3 | async-start | bytes 655360 | tf_op jit(solution)/shard_map/while/body/eval_jaxpr/reduce_scatter | solution.py:156
  467.0 3.6 copy-start.8
  467.0 5.4 copy-start.14
  467.0 4.5 collective-permute-start
  472.3 12.4 copy-start.13
  472.3 114.2 %reduce-scatter.5.cloned.1.call-start = ((), (), s32[]{:S(2)}) async-start(), calls=%async_computation.3 | async-start | bytes 655360 | tf_op jit(solution)/shard_map/while/body/eval_jaxpr/reduce_scatter | solution.py:156
  587.6 3.6 copy-start.8
  587.6 5.4 copy-start.14
  587.6 4.5 collective-permute-start
  593.0 12.4 copy-start.13
  593.0 112.6 %reduce-scatter.5.cloned.1.call-start = ((), (), s32[]{:S(2)}) async-start(), calls=%async_computation.3 | async-start | bytes 655360 | tf_op jit(solution)/shard_map/while/body/eval_jaxpr/reduce_scatter | solution.py:156
  706.6 3.6 copy-start.8
  706.6 5.4 copy-start.14
  706.6 4.5 collective-permute-start
  712.0 12.4 copy-start.13
  712.0 113.3 %reduce-scatter.5.cloned.1.call-start = ((), (), s32[]{:S(2)}) async-start(), calls=%async_computation.3 | async-start | bytes 655360 | tf_op jit(solution)/shard_map/while/body/eval_jaxpr/reduce_scatter | solution.py:156
  826.3 15.2 %copy-start.14 = (pred[2,64,256]{2,1,0:T(8,128)(4,1)S(1)}, pred[2,64,256]{2,1,0:T(8,128)(4,1)}, u32[]{:S(2)}) copy-start(pred[2,64,256]{2,1,0:T(8,128)(4,1)} %copy-done.13) | copy-start | bytes 98308 | tf_op jit(solution)/shard_map/while
  826.3 14.3 %collective-permute-start = (bf16[64,6144]{1,0:T(8,128)(2,1)}, bf16[64,6144]{1,0:T(8,128)(2,1)S(1)}, u32[]{:S(2)}, u32[]{:S(2)}) collective-permute-start(bf16[64,6144]{1,0:T(8,128)(2,1)} %get-tuple-element.464), channel_id=1, source_target_pairs={{4,0},{8,4},{12,8},{16,12},{20,16},{24,20},{28,24},{5,1},{9,5},{13... | collective-permute-start | bytes 2359304 | tf_op jit(solution)/shard_map/while/body/eval_jaxpr/ppermute | solution.py:17
  830.0 10.7 copy-start.9
  841.5 20.7 %copy-start.13 = (pred[2,64,256]{2,1,0:T(8,128)(4,1)}, pred[2,64,256]{2,1,0:T(8,128)(4,1)S(1)}, u32[]{:S(2)}) copy-start(pred[2,64,256]{2,1,0:T(8,128)(4,1)S(1)} %get-tuple-element.519) | copy-start | bytes 98308 | tf_op jit(solution)/shard_map/while
  841.5 101.8 %reduce-scatter.5.cloned.1.call-start = ((), (), s32[]{:S(2)}) async-start(), calls=%async_computation.3 | async-start | bytes 655360 | tf_op jit(solution)/shard_map/while/body/eval_jaxpr/reduce_scatter | solution.py:156
  862.3 15.8 %copy-start.2 = (bf16[256,1024]{1,0:T(8,128)(2,1)}, bf16[256,1024]{1,0:T(8,128)(2,1)S(1)}, u32[]{:S(2)}) copy-start(bf16[256,1024]{1,0:T(8,128)(2,1)S(1)} %get-tuple-element.292) | copy-start | bytes 1572868 | tf_op jit(solution)/shard_map/while/body/eval_jaxpr/cond
  864.7 19.9 %copy-start.5 = (bf16[8,12,8,128]{3,2,1,0:T(8,128)(2,1)}, bf16[8,12,8,128]{3,2,1,0:T(8,128)(2,1)S(1)}, u32[]{:S(2)}) copy-start(bf16[8,12,8,128]{3,2,1,0:T(8,128)(2,1)S(1)} %get-tuple-element.373) | copy-start | bytes 589828 | tf_op jit(solution)/shard_map/while/body/eval_jaxpr/cond
  954.9 5.4 copy-start.14
  954.9 4.5 collective-permute-start
  960.3 21.4 %copy-start.13 = (pred[2,64,256]{2,1,0:T(8,128)(4,1)}, pred[2,64,256]{2,1,0:T(8,128)(4,1)S(1)}, u32[]{:S(2)}) copy-start(pred[2,64,256]{2,1,0:T(8,128)(4,1)S(1)} %get-tuple-element.519) | copy-start | bytes 98308 | tf_op jit(solution)/shard_map/while
  960.3 95.1 %reduce-scatter.5.cloned.1.call-start = ((), (), s32[]{:S(2)}) async-start(), calls=%async_computation.3 | async-start | bytes 655360 | tf_op jit(solution)/shard_map/while/body/eval_jaxpr/reduce_scatter | solution.py:156
  981.7 15.8 %copy-start.2 = (bf16[256,1024]{1,0:T(8,128)(2,1)}, bf16[256,1024]{1,0:T(8,128)(2,1)S(1)}, u32[]{:S(2)}) copy-start(bf16[256,1024]{1,0:T(8,128)(2,1)S(1)} %get-tuple-element.292) | copy-start | bytes 1572868 | tf_op jit(solution)/shard_map/while/body/eval_jaxpr/cond
  984.1 19.9 %copy-start.5 = (bf16[8,12,8,128]{3,2,1,0:T(8,128)(2,1)}, bf16[8,12,8,128]{3,2,1,0:T(8,128)(2,1)S(1)}, u32[]{:S(2)}) copy-start(bf16[8,12,8,128]{3,2,1,0:T(8,128)(2,1)S(1)} %get-tuple-element.373) | copy-start | bytes 589828 | tf_op jit(solution)/shard_map/while/body/eval_jaxpr/cond
  1067.0 5.4 copy-start.14
  1067.0 4.5 collective-permute-start
  1072.4 232.3 %reduce-scatter.3.cloned.1.call-start = ((), (), s32[]{:S(2)}) async-start(), calls=%async_computation.2 | async-start | bytes 31457280 | tf_op jit(solution)/shard_map/reduce_scatter | solution.py:185
  (48 other events, 96.7 us)
Sparse Core Ops, SparseCore 0:
  33.1 77.9 reduce-scatter.4
  134.3 90.1 reduce-scatter.4
  247.6 98.3 reduce-scatter.4
  369.2 96.7 reduce-scatter.4
  489.1 97.4 reduce-scatter.4
  609.7 95.8 reduce-scatter.4
  728.7 96.5 reduce-scatter.4
  913.9 29.3 reduce-scatter.4
  1033.4 22.0 reduce-scatter.4
Sparse Core Ops, SparseCore 1:
  1085.7 218.9 reduce-scatter.2
where the time goes:
time: 1320 us
  waiting for transfers between devices  921 us (70%)
  matrix products  135 us (10%)
  blocking collectives  91.8 us (7%)
  other arithmetic  71.1 us (5%)
  local copies, waits for them, and re-layouts  69.4 us (5%)
  between operations  15.2 us (1%)
    reduce_scatter x9, waiting for transfers between devices, advance(): lax.psum_scatter(partial_terms.astype(jnp.bfloat16), 'dp', scatter_dimens...  684 us
    reduce_scatter x1, waiting for transfers between devices, shards(): lax.psum_scatter(partial_grad, 'dp', scatter_dimension=0, tiled=True)  219 us
    all_gather x9, blocking collectives, advance(): keyval_all = lax.all_gather(keyval, 'dp', axis=0, tiled=True)  91.8 us
    select_n x27, other arithmetic, store_at(): jnp.where(active, lax.dynamic_update_index_in_dim(store, fresh, slot, 0),...  42 us
    another operation x38, local copies, waits for them, and re-layouts  31.7 us
    dot_general x8, matrix products, attend_pass(): jnp.einsum('hqk,qhd->kd', soft_rounded, heads_up, preferred_element_type=...  26.5 us
  transfers between devices with their start and end apart: 19, of which 19 were waited for; matrix products, arithmetic and copies ran while one was open for 3% of the time, Pallas kernels for 0%

commit v1 on v0

v1 whole, which is shorter than its diff:
```python
import functools
import math

import jax
import jax.numpy as jnp
from jax import lax
from jax.experimental import pallas as pl
from jax.experimental.pallas import tpu as pltpu
from jax.sharding import PartitionSpec as P

H = 48
DH = 128
KVH = 4
TILE = 128
GROUP = H // KVH
SCALE = 1.0 / math.sqrt(DH)
MESH = pl.DeviceIdType.MESH
NT_DIMS = (((1,), (1,)), ((), ()))
TN_DIMS = (((0,), (0,)), ((), ()))


def relay(
    sections, ranks, micros, tokens,
    top, stream, normed, inverse, gain, weight, keyval, probs, attn, keyval_raw, normed_t,
    grads, wgrad,
    up, part, landed, dquery, total, dkv, dkv_all, mean,
    up_send, up_recv, part_send, part_recv, dkv_send, dkv_recv,
):
    sec = lax.axis_index("section")
    me = lax.axis_index("dp")
    width = GROUP * DH
    model = width * KVH

    barrier = pltpu.get_barrier_semaphore()
    for step in (1, sections - 1):
        pl.semaphore_signal(
            barrier, inc=1, device_id=(lax.rem(sec + step, sections), me), device_id_type=MESH
        )
    for step in range(1, ranks):
        pl.semaphore_signal(
            barrier, inc=1, device_id=(sec, lax.rem(me + step, ranks)), device_id_type=MESH
        )
    pl.semaphore_wait(barrier, 2 + ranks - 1)

    @pl.when(sec == sections - 1)
    def _():
        up[...] = top[...]

    def cols(g):
        return pl.ds(pl.multiple_of(g * width, 128), width)

    def up_copy(m, g):
        return pltpu.make_async_remote_copy(
            src_ref=grads.at[m, :, cols(g)],
            dst_ref=up.at[m, :, cols(g)],
            send_sem=up_send.at[m, g],
            recv_sem=up_recv.at[m, g],
            device_id=(lax.rem(sec + sections - 1, sections), me),
            device_id_type=MESH,
        )

    def part_copy(m, g, slot, peer):
        rows = pl.ds(pl.multiple_of(peer * tokens, tokens), tokens)
        return pltpu.make_async_remote_copy(
            src_ref=part.at[m, g, rows, :],
            dst_ref=landed.at[m, g, slot],
            send_sem=part_send.at[m, g, slot],
            recv_sem=part_recv.at[m, g, slot],
            device_id=(sec, peer),
            device_id_type=MESH,
        )

    def dkv_copy(m, step):
        return pltpu.make_async_remote_copy(
            src_ref=dkv.at[m],
            dst_ref=dkv_all.at[m, step],
            send_sem=dkv_send.at[m, step],
            recv_sem=dkv_recv.at[m, step],
            device_id=(sec, lax.rem(me + step + 1, ranks)),
            device_id_type=MESH,
        )

    def stacked(block):
        return jnp.concatenate([block[:, h * DH : (h + 1) * DH] for h in range(GROUP)], axis=0)

    def attend(m, g):
        @pl.when(sec < sections - 1)
        def _():
            up_copy(m, g).wait_recv()

        ups = stacked(up[m, :, cols(g)])
        queries = stacked(normed[m, :, cols(g)])
        keys = keyval[m, :, pl.ds(pl.multiple_of(g * DH, DH), DH)]
        values = keyval[m, :, pl.ds(pl.multiple_of((KVH + g) * DH, DH), DH)]
        delta = jnp.sum(
            ups.astype(jnp.float32) * attn[m, g].astype(jnp.float32), axis=-1, keepdims=True
        )
        soft = probs[m, g]
        part[m, g, :, DH:] = lax.dot_general(
            soft.astype(jnp.bfloat16), ups, TN_DIMS, preferred_element_type=jnp.float32
        ).astype(jnp.bfloat16)
        dprobs = lax.dot_general(ups, values, NT_DIMS, preferred_element_type=jnp.float32)
        dscores = (soft * (dprobs - delta) * SCALE).astype(jnp.bfloat16)
        part[m, g, :, :DH] = lax.dot_general(
            dscores, queries, TN_DIMS, preferred_element_type=jnp.float32
        ).astype(jnp.bfloat16)
        for step in range(1, ranks):

            @pl.when(me >= step)
            def _():
                part_copy(m, g, step - 1, lax.max(me - step, 0)).start()

        dq = jnp.dot(dscores, keys, preferred_element_type=jnp.float32)
        dq = jnp.concatenate([dq[h * tokens : (h + 1) * tokens] for h in range(GROUP)], axis=1)
        dquery[:, cols(g)] = dq
        weighed = stream[m, :, cols(g)].astype(jnp.float32) * gain[:, cols(g)]
        mean[...] += jnp.sum(weighed * dq, axis=-1, keepdims=True)

    def gather(m, g):
        rows = pl.ds(pl.multiple_of(me * tokens, tokens), tokens)
        total[...] = part[m, g, rows, :].astype(jnp.float32)
        for step in range(1, ranks):

            @pl.when(me < ranks - step)
            def _():
                part_copy(m, g, step - 1, lax.max(me - step, 0)).wait_recv()
                total[...] += landed[m, g, step - 1].astype(jnp.float32)

        rounded = total[...].astype(jnp.bfloat16)
        key_cols = pl.ds(pl.multiple_of(g * DH, DH), DH)
        value_cols = pl.ds(pl.multiple_of((KVH + g) * DH, DH), DH)
        dkv[m, :, key_cols] = rounded[:, :DH]
        dkv[m, :, value_cols] = rounded[:, DH:]
        wide = rounded.astype(jnp.float32)
        mean[...] += jnp.sum(
            wide[:, :DH] * keyval_raw[m, :, key_cols] + wide[:, DH:] * keyval_raw[m, :, value_cols],
            axis=-1,
            keepdims=True,
        )

    def project(m, g):
        back = lax.dot_general(
            dkv[m], weight[cols(g), :], NT_DIMS, preferred_element_type=jnp.float32
        )
        scaled = gain[:, cols(g)] * (dquery[:, cols(g)] + back)
        inv = inverse[m]
        pull = inv * inv * inv * (mean[...] * (1.0 / model))
        fresh = (
            up[m, :, cols(g)].astype(jnp.float32)
            + inv * scaled
            - stream[m, :, cols(g)].astype(jnp.float32) * pull
        )
        grads[m, :, cols(g)] = fresh.astype(jnp.bfloat16)

        @pl.when(sec > 0)
        def _():
            up_copy(m, g).start()

    def one_micro(m, carry):
        mean[...] = jnp.zeros_like(mean)
        pl.loop(0, KVH)(functools.partial(attend, m))
        pl.loop(0, KVH)(functools.partial(gather, m))
        for step in range(ranks - 1):
            dkv_copy(m, step).start()
        pl.loop(0, KVH)(functools.partial(project, m))
        return carry

    lax.fori_loop(0, micros, one_micro, 0)

    for m in range(micros):
        for step in range(ranks - 1):
            dkv_copy(m, step).wait_recv()

    rows = wgrad.shape[0]
    block = 256 if rows % 256 == 0 else rows

    @pl.loop(0, rows // block)
    def _(i):
        here = pl.ds(pl.multiple_of(i * block, block), block)
        acc = jnp.zeros((block, wgrad.shape[1]), jnp.float32)
        for m in range(micros):
            terms = jnp.concatenate([dkv[m]] + [dkv_all[m, s] for s in range(ranks - 1)], axis=0)
            acc += jnp.dot(normed_t[m, here, :], terms, preferred_element_type=jnp.float32)
        wgrad[here, :] = acc.astype(jnp.bfloat16)

    for m in range(micros):
        for step in range(ranks - 1):
            dkv_copy(m, step).wait_send()

    def drain(m, carry):
        def drain_group(g):
            @pl.when(sec > 0)
            def _():
                up_copy(m, g).wait_send()

            for step in range(1, ranks):

                @pl.when(me >= step)
                def _():
                    part_copy(m, g, step - 1, lax.max(me - step, 0)).wait_send()

        pl.loop(0, KVH)(drain_group)
        return carry

    lax.fori_loop(0, micros, drain, 0)


def shards(stream_in, gain, kv_weight, pattern, top_grad):
    sections = lax.axis_size("section")
    ranks = lax.axis_size("dp")
    rank = lax.axis_index("dp")
    stream = stream_in[0]
    micros, tokens, model = stream.shape
    weight = kv_weight[0]
    kv_width = weight.shape[1] // 2
    seq = tokens * ranks
    gain_f = gain.astype(jnp.float32)

    stream_f = stream.astype(jnp.float32)
    inverse = lax.rsqrt(jnp.mean(stream_f * stream_f, axis=-1, keepdims=True) + 1e-05)
    normed = (stream_f * inverse * gain_f[None]).astype(jnp.bfloat16)
    raw = jnp.dot(
        normed.reshape(micros * tokens, model), weight, preferred_element_type=jnp.float32
    ).reshape(micros, tokens, 2 * kv_width)
    keyval = lax.all_gather(raw.astype(jnp.bfloat16), "dp", axis=1, tiled=True)
    owned = lax.all_to_all(normed, "dp", split_axis=2, concat_axis=1, tiled=True)
    owned = owned.reshape(micros, ranks, tokens, model // ranks)
    order = lax.rem(rank - jnp.arange(ranks) + ranks, ranks)
    owned = jnp.take(owned, order, axis=1).reshape(micros, seq, model // ranks)
    normed_t = jnp.swapaxes(owned, 1, 2)

    tiles = seq // TILE
    query_pos = rank * tokens + jnp.arange(tokens)
    key_pos = jnp.arange(seq)
    seen = jnp.zeros((micros, tokens, seq), jnp.bool_)
    for row in range(tiles):
        for col in range(row + 1):
            pair = (query_pos[:, None] // TILE == row) & (key_pos[None, :] // TILE == col)
            seen = seen | (pair[None] & (pattern[:, row, col] > 0)[:, None, None])
    allowed = seen & (key_pos[None, :] <= query_pos[:, None])[None]

    queries = jnp.transpose(
        normed.reshape(micros, tokens, KVH, GROUP, DH), (0, 2, 3, 1, 4)
    ).reshape(micros, KVH, GROUP * tokens, DH)
    heads = keyval.reshape(micros, seq, 2, KVH, DH)
    scores = (
        jnp.einsum("mgqd,mkgd->mgqk", queries, heads[:, :, 0], preferred_element_type=jnp.float32)
        * SCALE
    ).reshape(micros, KVH, GROUP, tokens, seq)
    scores = jnp.where(allowed[:, None, None], scores, -1e30)
    expo = jnp.exp(scores - jnp.max(scores, axis=-1, keepdims=True))
    probs = (expo / jnp.sum(expo, axis=-1, keepdims=True)).reshape(
        micros, KVH, GROUP * tokens, seq
    )
    attn = jnp.einsum(
        "mgqk,mkgd->mgqd",
        probs.astype(jnp.bfloat16),
        heads[:, :, 1],
        preferred_element_type=jnp.float32,
    ).astype(jnp.bfloat16)

    vmem = pl.BlockSpec(memory_space=pltpu.VMEM)
    bf16, f32 = jnp.bfloat16, jnp.float32
    grads, wgrad = pl.pallas_call(
        functools.partial(relay, sections, ranks, micros, tokens),
        out_shape=(
            jax.ShapeDtypeStruct((micros, tokens, model), bf16),
            jax.ShapeDtypeStruct((model // ranks, 2 * kv_width), bf16),
        ),
        in_specs=[vmem] * 11,
        out_specs=(vmem, vmem),
        scratch_shapes=[
            pltpu.VMEM((micros, tokens, model), bf16),
            pltpu.VMEM((micros, KVH, seq, 2 * DH), bf16),
            pltpu.VMEM((micros, KVH, ranks - 1, tokens, 2 * DH), bf16),
            pltpu.VMEM((tokens, model), f32),
            pltpu.VMEM((tokens, 2 * DH), f32),
            pltpu.VMEM((micros, tokens, 2 * kv_width), bf16),
            pltpu.VMEM((micros, ranks - 1, tokens, 2 * kv_width), bf16),
            pltpu.VMEM((tokens, 1), f32),
            pltpu.SemaphoreType.DMA((micros, KVH)),
            pltpu.SemaphoreType.DMA((micros, KVH)),
            pltpu.SemaphoreType.DMA((micros, KVH, ranks - 1)),
            pltpu.SemaphoreType.DMA((micros, KVH, ranks - 1)),
            pltpu.SemaphoreType.DMA((micros, ranks - 1)),
            pltpu.SemaphoreType.DMA((micros, ranks - 1)),
        ],
        compiler_params=pltpu.CompilerParams(
            collective_id=0, has_side_effects=True, vmem_limit_bytes=60 * 1024 * 1024
        ),
    )(
        top_grad, stream, normed, inverse, gain_f, weight, keyval, probs, attn, raw / inverse,
        normed_t,
    )
    return grads[None], wgrad[None]


def solution(mesh):
    placed = (
        P("section", None, "dp", None),
        P("section", None),
        P("section", None, None),
        P(),
        P(None, "dp", None),
    )
    return jax.shard_map(
        shards,
        mesh=mesh,
        in_specs=placed,
        out_specs=(P("section", None, "dp", None), P("section", "dp", None)),
        check_vma=False,
    )
```

time: 1320 us -> 208 us (0.16)
  waiting for transfers between devices: 921 us -> 16.8 us
  matrix products: 135 us -> 11.5 us
  Pallas kernels: 0 us -> 112 us
  blocking collectives: 91.8 us -> 0 us
  other arithmetic: 71.1 us -> 12.5 us
  local copies, waits for them, and re-layouts: 69.4 us -> 35.1 us
    reduce_scatter x10 -> x0, waiting for transfers between devices: 903 us -> none  [the longest x9 684 us: advance(): lax.psum_scatter(partial_terms.astype(jnp.bfloat16), 'dp', scatter_dimens...]
    pallas_call x0 -> x1, Pallas kernels: none -> 112 us  [shards(): pl.pallas_call(functools.partial(relay, sections, ranks, micros, tokens),...]
    dot_general x46 -> x3, matrix products: 118 us -> 11.5 us  [the longest x1 7.92 us: shards(): jnp.dot(normed.reshape(micros * tokens, model), weight, preferred_element...]
    all_gather x9 -> x0, blocking collectives: 91.8 us -> none  [advance(): keyval_all = lax.all_gather(keyval, 'dp', axis=0, tiled=True)]
    select_n x38 -> x1, other arithmetic: 55.2 us -> 0.01 us  [shards(): owned = jnp.take(owned, order, axis=1).reshape(micros, seq, model // ranks)]
    another operation x38 -> x0, local copies, waits for them, and re-layouts: 31.7 us -> none
    cond x57 -> x0, local copies, waits for them, and re-layouts: 28.3 us -> none  [the longest x9 18.5 us: advance(): lax.cond(active, attend_pass, attend_skip, (normalized_rows, keyval_all,...]
    ppermute x9 -> x0, waiting for transfers between devices: 17.3 us -> none  [from_behind(): return lax.ppermute(x, axis, pairs)]
  transfers between devices with their start and end apart: 19 -> 2, of which waited for: 19 -> 1; matrix products, arithmetic and copies ran while one was open for 3% -> 16% of each run, Pallas kernels for 0% -> 0%
where the time goes in v1:
time: 208 us; the launch traced here: 207 us
  Pallas kernels  112 us (54%)
  local copies, waits for them, and re-layouts  35.1 us (17%)
  waiting for transfers between devices  16.8 us (8%)
  between operations  14.3 us (7%)
  other arithmetic  12.5 us (6%)
  matrix products  11.5 us (6%)
  starting transfers between devices  5.22 us (3%)
    pallas_call x1, Pallas kernels, shards(): pl.pallas_call(functools.partial(relay, sections, ranks, micros, tokens),...  112 us
    all_to_all x1, waiting for transfers between devices, shards(): lax.all_to_all(normed, 'dp', split_axis=2, concat_axis=1, tiled=True)  16.8 us
    unnamed x20, local copies, waits for them, and re-layouts  13.9 us
    dot_general x1, matrix products, shards(): jnp.dot(normed.reshape(micros * tokens, model), weight, preferred_element...  7.92 us
    convert_element_type x1, local copies, waits for them, and re-layouts, shards(): normed = (stream_f * inverse * gain_f[None]).astype(jnp.bfloat16)  5.32 us
    all_to_all x1, local copies, waits for them, and re-layouts, shards(): lax.all_to_all(normed, 'dp', split_axis=2, concat_axis=1, tiled=True)  5.26 us
    all_to_all x1, starting transfers between devices, shards(): lax.all_to_all(normed, 'dp', split_axis=2, concat_axis=1, tiled=True)  5.18 us
  transfers between devices with their start and end apart: 2, of which 1 were waited for; matrix products, arithmetic and copies ran while one was open for 16% of the time, Pallas kernels for 0%

profile of v1, /device:TPU:0, one launch (start us, length us, event | category | flops | bytes accessed | tf_op | source)
XLA Modules:
  0.0 207.1 jit_solution(7343884758604199232)
XLA Ops:
  7.2 0.0 all-gather.2.cloned.1.call-start
  7.2 1.8 fusion.4
  9.0 0.8 convert_element_type.40.gain
  9.8 0.0 copy-start.5
  9.8 0.0 copy-start.1
  9.8 7.9 %broadcast_divide_fusion.1 = (f32[2,64,1024]{2,1,0:T(8,128)}, bf16[2,64,1024]{2,1,0:T(8,128)(2,1)}) fusion(f32[2,64]{1,0:T(2,128)S(1)} %get-tuple-element.14, bf16[1,6144,1024]{2,1,0:T(8,128)(2,1)} %param.7, f32[6144]{0:T(1024)S(1)} %bitcast.53, bf16[1,2,64,6144]{3,2,1,0:T(8,128)(2,1)} %param.5), kind=kOutput, calls=%fused_computation.30 | convolution fusion | flops 1614020608 | bytes 14967296 | tf_op jit(solution)/shard_map/dot_general | solution.py:222
  17.7 0.0 all-gather.2.cloned.1.call-update
  17.8 0.0 copy-done.5
  17.8 0.0 copy-done.1
  17.8 0.4 fusion.6.normed
  18.2 0.0 copy-start.2
  18.3 5.3 %copy.39 = bf16[2,64,6144]{1,0,2:T(2,128)(2,1)} copy(bf16[2,64,6144]{2,1,0:T(8,128)(2,1)S(1)} %fusion.6.normed) | data formatting | bytes 3145728 | tf_op jit(solution)/shard_map/convert_element_type | solution.py:221
  23.6 5.1 %reshape.344 = bf16[4,2,98304]{2,1,0:T(2,128)(2,1)} reshape(bf16[6144,2,64]{2,1,0:T(2,128)(2,1)} %bitcast.45) | data formatting | bytes 3145728
  28.6 0.0 copy-done.2
  28.7 5.2 %all-to-all-start = ((bf16[4,2,98304]{2,1,0:T(2,128)(2,1)}), bf16[4,2,98304]{2,1,0:T(2,128)(2,1)}, u32[]{:S(2)}, u32[]{:S(2)}) async-start(bf16[4,2,98304]{2,1,0:T(2,128)(2,1)} %reshape.344), calls=%async_computation | async-start | bytes 3145728 | tf_op jit(solution)/shard_map/all_to_all | solution.py:226
  33.9 2.4 %reshape.324 = f32[2,64,4,12,128]{4,3,2,1,0:T(8,128)} reshape(bf16[1,2,64,6144]{3,2,1,0:T(8,128)(2,1)S(1)} %copy-done.1) | data formatting | bytes 4718592 | tf_op jit(solution)/shard_map/convert_element_type | solution.py:219
  36.3 0.1 convert_reduce_fusion
  36.4 2.7 %fusion.12 = bf16[2,4,12,64,128]{4,2,1,3,0:T(8,128)(2,1)S(1)} fusion(f32[2,64,4,12,128]{4,3,2,1,0:T(8,128)} %reshape.324, f32[4,12,128]{2,1,0:T(8,128)S(1)} %mul.77, f32[2,64]{1,0:T(2,128)S(1)} %get-tuple-element.14), kind=kLoop, calls=%fused_computation.20 | loop fusion | flops 2359296 | bytes 4743680 | tf_op jit(solution)/shard_map/transpose | solution.py:242
  39.1 0.0 copy-start.7
  39.2 2.2 %copy.35 = bf16[2,4,12,64,128]{4,3,2,1,0:T(8,128)(2,1)} copy(bf16[2,4,12,64,128]{4,2,1,3,0:T(8,128)(2,1)S(1)} %fusion.12) | data formatting | bytes 3145728 | tf_op jit(solution)/shard_map/transpose | solution.py:242
  41.3 0.1 broadcast_in_dim.60
  41.4 0.1 broadcast_in_dim.61
  41.5 0.7 copy.44.inverse
  42.2 0.0 copy-done.7
  42.2 0.2 compare_reduce_fusion.2
  42.5 0.1 iota_compare_fusion
  42.6 0.1 broadcast_and_fusion.2
  42.7 0.1 or_and_fusion
  42.8 16.8 %all-to-all-done = bf16[4,2,98304]{2,1,0:T(2,128)(2,1)} async-done(((bf16[4,2,98304]{2,1,0:T(2,128)(2,1)}), bf16[4,2,98304]{2,1,0:T(2,128)(2,1)}, u32[]{:S(2)}, u32[]{:S(2)}) %all-to-all-start) | async-done | bytes 1572896 | tf_op jit(solution)/shard_map/all_to_all | solution.py:226
  59.6 3.8 %reshape.345 = bf16[6144,2,64]{2,1,0:T(2,128)(2,1)S(1)} reshape(bf16[4,2,98304]{2,1,0:T(2,128)(2,1)} %all-to-all-done) | data formatting | bytes 3145728
  63.4 5.3 %copy.41 = bf16[2,64,4,1536]{3,1,2,0:T(8,128)(2,1)} copy(bf16[2,64,4,1536]{1,0,3,2:T(2,128)(2,1)S(1)} %bitcast.44) | data formatting | bytes 3145728 | tf_op jit(solution)/shard_map/all_to_all | solution.py:226
  68.7 2.1 gather_fusion
  70.7 0.1 copy.42
  70.8 0.7 copy.43
  71.5 0.0 copy-start.3
  71.5 1.3 select_bitcast_fusion.normed_t
  72.9 1.8 reshape.323
  74.7 0.4 fusion.28
  75.0 1.0 fusion.21
  76.0 0.2 broadcast_in_dim.34
  76.2 3.7 %fusion.29 = (f32[2,4,768]{2,1,0:T(4,128)S(1)}, f32[2,4,768,256]{3,2,1,0:T(8,128)S(1)}) fusion(f32[2,4,768,256]{3,2,1,0:T(8,128)S(1)} %fusion.21, pred[2,768,256]{2,1,0:T(8,128)(4,1)S(1)} %bitcast.52), kind=kOutput, calls=%fused_computation.69 | output fusion | flops 9437439 | bytes 13000704 | tf_op jit(solution)/shard_map/sub | solution.py:251
  79.9 1.1 broadcast_divide_fusion.probs
  81.0 2.6 %fusion.13.attn = bf16[2,4,768,128]{3,2,1,0:T(8,128)(2,1)} fusion(f32[2,4,768,256]{3,2,1,0:T(8,128)S(1)} %broadcast_divide_fusion.probs, bf16[2,256,1,4,128]{4,3,2,1,0:T(4,128)(2,1)S(1)} %get-tuple-element.9), kind=kOutput, calls=%fused_computation.21 | convolution fusion | flops 405012480 | bytes 8388608 | tf_op jit(solution)/shard_map/mgqk,mkgd->mgqd/dot_general | solution.py:255
  83.6 0.5 copy-done
  84.1 111.7 %shard_map.68 = (bf16[2,64,6144]{2,1,0:T(8,128)(2,1)}, bf16[1536,1024]{1,0:T(8,128)(2,1)}) custom-call(bf16[2,64,6144]{2,1,0:T(8,128)(2,1)} %top.1, bf16[2,64,6144]{2,1,0:T(8,128)(2,1)} %bitcast.42, bf16[2,64,6144]{2,1,0:T(8,128)(2,1)} %copy-done.2, f32[2,64,1]{2,1,0:T(8,128)} %copy.44.inverse, f32[1,6144]{1,0:T(1,128)} %copy-done.5, ...), custom_call_target="tpu_custom_call" | custom-call | tf_op jit(solution)/shard_map/pallas_call | solution.py:264
  195.8 2.8 %copy.56 = bf16[1,2,64,6144]{3,2,1,0:T(8,128)(2,1)} copy(bf16[1,2,64,6144]{3,2,1,0:T(8,128)(2,1)} %bitcast.51) | data formatting | bytes 3145728
  198.6 0.0 copy-done.4
  198.6 1.7 copy.57
  (14 shorter events, 0.1 us)
Async XLA Ops:
  7.2 65.7 %all-gather.2.cloned.1.call-start = ((), (), s32[]{:S(2)}) async-start(), calls=%async_computation.1 | async-start | bytes 1310720 | tf_op jit(solution)/shard_map/all_gather | solution.py:225
  9.8 8.0 %copy-start.5 = (f32[1,6144]{1,0:T(1,128)}, f32[1,6144]{1,0:T(1,128)S(1)}, u32[]{:S(2)}) copy-start(f32[1,6144]{1,0:T(1,128)S(1)} %convert_element_type.40.gain) | copy-start | bytes 73732
  9.8 8.0 %copy-start.1 = (bf16[1,2,64,6144]{3,2,1,0:T(8,128)(2,1)S(1)}, bf16[1,2,64,6144]{3,2,1,0:T(8,128)(2,1)}, u32[]{:S(2)}) copy-start(bf16[1,2,64,6144]{3,2,1,0:T(8,128)(2,1)} %param.5) | copy-start | bytes 4718596
  18.2 10.4 %copy-start.2 = (bf16[2,64,6144]{2,1,0:T(8,128)(2,1)}, bf16[2,64,6144]{2,1,0:T(8,128)(2,1)S(1)}, u32[]{:S(2)}) copy-start(bf16[2,64,6144]{2,1,0:T(8,128)(2,1)S(1)} %fusion.6.normed) | copy-start | bytes 4718596
  28.7 31.0 %all-to-all-start = ((bf16[4,2,98304]{2,1,0:T(2,128)(2,1)}), bf16[4,2,98304]{2,1,0:T(2,128)(2,1)}, u32[]{:S(2)}, u32[]{:S(2)}) async-start(bf16[4,2,98304]{2,1,0:T(2,128)(2,1)} %reshape.344), calls=%async_computation | async-start | bytes 3145728 | tf_op jit(solution)/shard_map/all_to_all | solution.py:226
  33.8 2.5 %copy-start.6 = (bf16[1,6144]{1,0:T(2,128)(2,1)S(1)}, bf16[1,6144]{1,0:T(2,128)(2,1)}, u32[]{:S(2)}) copy-start(bf16[1,6144]{1,0:T(2,128)(2,1)} %param.6) | copy-start | bytes 36868
  39.1 3.1 %copy-start.7 = (s32[2,2,2]{2,1,0:T(2,128)S(1)}, s32[2,2,2]{2,1,0:T(2,128)}, u32[]{:S(2)}) copy-start(s32[2,2,2]{2,1,0:T(2,128)} %param.8) | copy-start | bytes 100
  71.5 3.5 %copy-start.3 = (bf16[2,4,12,64,128]{4,3,2,1,0:T(8,128)(2,1)S(1)}, bf16[2,4,12,64,128]{4,3,2,1,0:T(8,128)(2,1)}, u32[]{:S(2)}) copy-start(bf16[2,4,12,64,128]{4,3,2,1,0:T(8,128)(2,1)} %copy.35) | copy-start | bytes 4718596
  81.0 3.1 %copy-start = (f32[2,4,768,256]{3,2,1,0:T(8,128)}, f32[2,4,768,256]{3,2,1,0:T(8,128)S(1)}, u32[]{:S(2)}) copy-start(f32[2,4,768,256]{3,2,1,0:T(8,128)S(1)} %broadcast_divide_fusion.probs) | copy-start | bytes 18874372
  195.8 2.9 %copy-start.4 = (bf16[1536,1024]{1,0:T(8,128)(2,1)S(1)}, bf16[1536,1024]{1,0:T(8,128)(2,1)}, u32[]{:S(2)}) copy-start(bf16[1536,1024]{1,0:T(8,128)(2,1)} %get-tuple-element.5) | copy-start | bytes 9437188
Sparse Core Ops, SparseCore 0:
  17.9 40.1 all-gather.1

commit v2 on v1

v2 whole, which is shorter than its diff:
```python
import functools
import math

import jax
import jax.numpy as jnp
from jax import lax
from jax.experimental import pallas as pl
from jax.experimental.pallas import tpu as pltpu
from jax.sharding import PartitionSpec as P

H = 48
DH = 128
KVH = 4
TILE = 128
GROUP = H // KVH
SCALE = 1.0 / math.sqrt(DH)
MESH = pl.DeviceIdType.MESH
NT_DIMS = (((1,), (1,)), ((), ()))
TN_DIMS = (((0,), (0,)), ((), ()))


def relay(
    sections, ranks, micros, tokens,
    top, stream, gain, weight_hbm, mask,
    grads, wgrad,
    weight, normed, inverse, keyval_own, keyval, keyval_raw, probs, attn, owned,
    up, part, landed, dquery, total, dkv_all, mean,
    weight_sem, keyval_send, keyval_recv, owned_send, owned_recv,
    up_send, up_recv, part_send, part_recv, dkv_send, dkv_recv,
):
    sec = lax.axis_index("section")
    me = lax.axis_index("dp")
    width = GROUP * DH
    model = width * KVH
    seq = ranks * tokens
    share = model // ranks
    f32, bf16 = jnp.float32, jnp.bfloat16

    def cols(g):
        return pl.ds(pl.multiple_of(g * width, 128), width)

    def key_cols(g):
        return pl.ds(pl.multiple_of(g * DH, DH), DH)

    def value_cols(g):
        return pl.ds(pl.multiple_of((KVH + g) * DH, DH), DH)

    def rank_rows(rank):
        return pl.ds(pl.multiple_of(rank * tokens, tokens), tokens)

    def share_cols(rank):
        return pl.ds(pl.multiple_of(rank * share, 128), share)

    def weight_copy(g):
        return pltpu.make_async_copy(
            weight_hbm.at[cols(g), :], weight.at[cols(g), :], weight_sem.at[g]
        )

    def keyval_copy(step):
        return pltpu.make_async_remote_copy(
            src_ref=keyval_own,
            dst_ref=keyval.at[:, rank_rows(me), :],
            send_sem=keyval_send.at[step - 1],
            recv_sem=keyval_recv.at[step - 1],
            device_id=(sec, lax.rem(me + step, ranks)),
            device_id_type=MESH,
        )

    def owned_copy(step):
        peer = lax.rem(me + step, ranks)
        return pltpu.make_async_remote_copy(
            src_ref=normed.at[:, :, share_cols(peer)],
            dst_ref=owned.at[:, step],
            send_sem=owned_send.at[step - 1],
            recv_sem=owned_recv.at[step - 1],
            device_id=(sec, peer),
            device_id_type=MESH,
        )

    def stacked(block):
        return jnp.concatenate([block[:, h * DH : (h + 1) * DH] for h in range(GROUP)], axis=0)

    barrier = pltpu.get_barrier_semaphore()
    for step in (1, sections - 1):
        pl.semaphore_signal(
            barrier, inc=1, device_id=(lax.rem(sec + step, sections), me), device_id_type=MESH
        )
    for step in range(1, ranks):
        pl.semaphore_signal(
            barrier, inc=1, device_id=(sec, lax.rem(me + step, ranks)), device_id_type=MESH
        )
    for g in range(KVH):
        weight_copy(g).start()

    def normalize(m, carry):
        mean[...] = jnp.zeros_like(mean)

        @pl.loop(0, KVH)
        def _(g):
            wide = stream[m, :, cols(g)].astype(f32)
            mean[...] += jnp.sum(wide * wide, axis=-1, keepdims=True)

        inverse[m] = lax.rsqrt(mean[...] * (1.0 / model) + 1e-05)

        @pl.loop(0, KVH)
        def _(g):
            wide = stream[m, :, cols(g)].astype(f32)
            normed[m, :, cols(g)] = (wide * inverse[m] * gain[:, cols(g)]).astype(bf16)

        return carry

    lax.fori_loop(0, micros, normalize, 0)
    keyval_raw[...] = jnp.zeros_like(keyval_raw)

    @pl.loop(0, KVH)
    def _(g):
        weight_copy(g).wait()
        rows = normed[:, :, cols(g)].reshape(micros * tokens, width)
        keyval_raw[...] += jnp.dot(
            rows, weight[cols(g), :], preferred_element_type=f32
        ).reshape(keyval_raw.shape)

    keyval_own[...] = keyval_raw[...].astype(bf16)
    pl.semaphore_wait(barrier, 2 + ranks - 1)
    for step in range(1, ranks):

        @pl.when(me < ranks - step)
        def _():
            keyval_copy(step).start()

    for m in range(micros):
        keyval_raw[m] = keyval_raw[m] / inverse[m]
        keyval[m, rank_rows(me), :] = keyval_own[m]
        owned[m, 0] = normed[m, :, share_cols(me)]
    for rank in range(1, ranks):

        @pl.when(me < rank)
        def _():
            keyval[:, rank * tokens : (rank + 1) * tokens, :] = jnp.zeros(
                (micros, tokens, keyval.shape[2]), bf16
            )

    for step in range(1, ranks):

        @pl.when(me >= step)
        def _():
            keyval_copy(step).wait_recv()

    @pl.when(sec < sections - 1)
    def _():
        for step in range(1, ranks):
            owned_copy(step).start()

    def forward(m, carry):
        @pl.loop(0, KVH)
        def _(g):
            queries = stacked(normed[m, :, cols(g)])
            scores = (
                lax.dot_general(
                    keyval[m, :, key_cols(g)], queries, NT_DIMS, preferred_element_type=f32
                )
                * SCALE
            )
            seen = jnp.concatenate([mask[m]] * (GROUP * tokens // mask.shape[2]), axis=1)
            scores = jnp.where(seen > 0.5, scores, -1e30)
            expo = jnp.exp(scores - jnp.max(scores, axis=0, keepdims=True))
            soft = expo / jnp.sum(expo, axis=0, keepdims=True)
            probs[m, g] = soft
            attn[m, g] = lax.dot_general(
                soft.astype(bf16), keyval[m, :, value_cols(g)], TN_DIMS, preferred_element_type=f32
            ).astype(bf16)

        return carry

    lax.fori_loop(0, micros, forward, 0)

    @pl.when(sec == sections - 1)
    def _():
        up[...] = top[...]

    def up_copy(m, g):
        return pltpu.make_async_remote_copy(
            src_ref=grads.at[m, :, cols(g)],
            dst_ref=up.at[m, :, cols(g)],
            send_sem=up_send.at[m, g],
            recv_sem=up_recv.at[m, g],
            device_id=(lax.rem(sec + sections - 1, sections), me),
            device_id_type=MESH,
        )

    def part_copy(m, g, slot, peer):
        return pltpu.make_async_remote_copy(
            src_ref=part.at[m, g, rank_rows(peer), :],
            dst_ref=landed.at[m, g, slot],
            send_sem=part_send.at[m, g, slot],
            recv_sem=part_recv.at[m, g, slot],
            device_id=(sec, peer),
            device_id_type=MESH,
        )

    def dkv_copy(m, step):
        return pltpu.make_async_remote_copy(
            src_ref=dkv_all.at[m, 0],
            dst_ref=dkv_all.at[m, step + 1],
            send_sem=dkv_send.at[m, step],
            recv_sem=dkv_recv.at[m, step],
            device_id=(sec, lax.rem(me + step + 1, ranks)),
            device_id_type=MESH,
        )

    def attend(m, g):
        @pl.when(sec < sections - 1)
        def _():
            up_copy(m, g).wait_recv()

        ups = stacked(up[m, :, cols(g)])
        queries = stacked(normed[m, :, cols(g)])
        keys = keyval[m, :, key_cols(g)]
        values = keyval[m, :, value_cols(g)]
        product = ups.astype(f32) * attn[m, g].astype(f32)
        high = product.astype(bf16)
        low = (product - high.astype(f32)).astype(bf16)
        delta = lax.dot_general(
            jnp.ones((16, 2 * DH), bf16),
            jnp.concatenate([high, low], axis=1),
            NT_DIMS,
            preferred_element_type=f32,
        )[:1]
        soft = probs[m, g]
        dprobs = lax.dot_general(values, ups, NT_DIMS, preferred_element_type=f32)
        dscores = (soft * (dprobs - delta) * SCALE).astype(bf16)
        part[m, g, :, DH:] = jnp.dot(
            soft.astype(bf16), ups, preferred_element_type=f32
        ).astype(bf16)
        part[m, g, :, :DH] = jnp.dot(dscores, queries, preferred_element_type=f32).astype(bf16)
        for step in range(1, ranks):

            @pl.when(me >= step)
            def _():
                part_copy(m, g, step - 1, lax.max(me - step, 0)).start()

        dq = lax.dot_general(dscores, keys, TN_DIMS, preferred_element_type=f32)
        dq = jnp.concatenate([dq[h * tokens : (h + 1) * tokens] for h in range(GROUP)], axis=1)
        dquery[:, cols(g)] = dq
        weighed = stream[m, :, cols(g)].astype(jnp.float32) * gain[:, cols(g)]
        mean[...] += jnp.sum(weighed * dq, axis=-1, keepdims=True)

    def gather(m, g):
        total[...] = part[m, g, rank_rows(me), :].astype(jnp.float32)
        for step in range(1, ranks):

            @pl.when(me < ranks - step)
            def _():
                part_copy(m, g, step - 1, lax.max(me - step, 0)).wait_recv()
                total[...] += landed[m, g, step - 1].astype(jnp.float32)

        rounded = total[...].astype(jnp.bfloat16)
        dkv_all[m, 0, :, key_cols(g)] = rounded[:, :DH]
        dkv_all[m, 0, :, value_cols(g)] = rounded[:, DH:]
        wide = rounded.astype(jnp.float32)
        mean[...] += jnp.sum(
            wide[:, :DH] * keyval_raw[m, :, key_cols(g)]
            + wide[:, DH:] * keyval_raw[m, :, value_cols(g)],
            axis=-1,
            keepdims=True,
        )

    def project(m, g):
        back = lax.dot_general(
            dkv_all[m, 0], weight[cols(g), :], NT_DIMS, preferred_element_type=jnp.float32
        )
        scaled = gain[:, cols(g)] * (dquery[:, cols(g)] + back)
        inv = inverse[m]
        pull = inv * inv * inv * (mean[...] * (1.0 / model))
        fresh = (
            up[m, :, cols(g)].astype(jnp.float32)
            + inv * scaled
            - stream[m, :, cols(g)].astype(jnp.float32) * pull
        )
        grads[m, :, cols(g)] = fresh.astype(jnp.bfloat16)

        @pl.when(sec > 0)
        def _():
            up_copy(m, g).start()

    def one_micro(m, carry):
        mean[...] = jnp.zeros_like(mean)
        pl.loop(0, KVH)(functools.partial(attend, m))
        pl.loop(0, KVH)(functools.partial(gather, m))
        for step in range(ranks - 1):
            dkv_copy(m, step).start()
        pl.loop(0, KVH)(functools.partial(project, m))
        return carry

    lax.fori_loop(0, micros, one_micro, 0)

    @pl.when(sec == sections - 1)
    def _():
        for step in range(1, ranks):
            owned_copy(step).start()

    for step in range(1, ranks):
        owned_copy(step).wait_recv()
    for m in range(micros):
        for step in range(ranks - 1):
            dkv_copy(m, step).wait_recv()

    block = 256 if share % 256 == 0 else share

    @pl.loop(0, share // block)
    def _(i):
        here = pl.ds(pl.multiple_of(i * block, block), block)
        wgrad[here, :] = lax.dot_general(
            owned[:, :, :, here].reshape(micros * seq, block),
            dkv_all[...].reshape(micros * seq, wgrad.shape[1]),
            TN_DIMS,
            preferred_element_type=f32,
        ).astype(bf16)

    for step in range(1, ranks):
        owned_copy(step).wait_send()

        @pl.when(me < ranks - step)
        def _():
            keyval_copy(step).wait_send()

    for m in range(micros):
        for step in range(ranks - 1):
            dkv_copy(m, step).wait_send()

    def drain(m, carry):
        def drain_group(g):
            @pl.when(sec > 0)
            def _():
                up_copy(m, g).wait_send()

            for step in range(1, ranks):

                @pl.when(me >= step)
                def _():
                    part_copy(m, g, step - 1, lax.max(me - step, 0)).wait_send()

        pl.loop(0, KVH)(drain_group)
        return carry

    lax.fori_loop(0, micros, drain, 0)


def shards(stream_in, gain, kv_weight, pattern, top_grad):
    sections = lax.axis_size("section")
    ranks = lax.axis_size("dp")
    rank = lax.axis_index("dp")
    stream = stream_in[0]
    micros, tokens, model = stream.shape
    weight = kv_weight[0]
    kv_width = weight.shape[1] // 2
    seq = tokens * ranks

    tiles = seq // TILE
    query_pos = rank * tokens + jnp.arange(tokens)
    key_pos = jnp.arange(seq)
    seen = jnp.zeros((micros, tokens, seq), jnp.bool_)
    for row in range(tiles):
        for col in range(row + 1):
            pair = (query_pos[:, None] // TILE == row) & (key_pos[None, :] // TILE == col)
            seen = seen | (pair[None] & (pattern[:, row, col] > 0)[:, None, None])
    allowed = seen & (key_pos[None, :] <= query_pos[:, None])[None]

    mask = jnp.swapaxes(allowed, 1, 2).astype(jnp.float32)
    mask = jnp.tile(mask, (1, 1, max(1, DH // tokens)))

    vmem = pl.BlockSpec(memory_space=pltpu.VMEM)
    bf16, f32 = jnp.bfloat16, jnp.float32
    grads, wgrad = pl.pallas_call(
        functools.partial(relay, sections, ranks, micros, tokens),
        out_shape=(
            jax.ShapeDtypeStruct((micros, tokens, model), bf16),
            jax.ShapeDtypeStruct((model // ranks, 2 * kv_width), bf16),
        ),
        in_specs=[vmem, vmem, vmem, pl.BlockSpec(memory_space=pl.ANY), vmem],
        out_specs=(vmem, vmem),
        scratch_shapes=[
            pltpu.VMEM((model, 2 * kv_width), bf16),
            pltpu.VMEM((micros, tokens, model), bf16),
            pltpu.VMEM((micros, tokens, 1), f32),
            pltpu.VMEM((micros, tokens, 2 * kv_width), bf16),
            pltpu.VMEM((micros, seq, 2 * kv_width), bf16),
            pltpu.VMEM((micros, tokens, 2 * kv_width), f32),
            pltpu.VMEM((micros, KVH, seq, GROUP * tokens), f32),
            pltpu.VMEM((micros, KVH, GROUP * tokens, DH), bf16),
            pltpu.VMEM((micros, ranks, tokens, model // ranks), bf16),
            pltpu.VMEM((micros, tokens, model), bf16),
            pltpu.VMEM((micros, KVH, seq, 2 * DH), bf16),
            pltpu.VMEM((micros, KVH, ranks - 1, tokens, 2 * DH), bf16),
            pltpu.VMEM((tokens, model), f32),
            pltpu.VMEM((tokens, 2 * DH), f32),
            pltpu.VMEM((micros, ranks, tokens, 2 * kv_width), bf16),
            pltpu.VMEM((tokens, 1), f32),
            pltpu.SemaphoreType.DMA((KVH,)),
            pltpu.SemaphoreType.DMA((ranks - 1,)),
            pltpu.SemaphoreType.DMA((ranks - 1,)),
            pltpu.SemaphoreType.DMA((ranks - 1,)),
            pltpu.SemaphoreType.DMA((ranks - 1,)),
            pltpu.SemaphoreType.DMA((micros, KVH)),
            pltpu.SemaphoreType.DMA((micros, KVH)),
            pltpu.SemaphoreType.DMA((micros, KVH, ranks - 1)),
            pltpu.SemaphoreType.DMA((micros, KVH, ranks - 1)),
            pltpu.SemaphoreType.DMA((micros, ranks - 1)),
            pltpu.SemaphoreType.DMA((micros, ranks - 1)),
        ],
        compiler_params=pltpu.CompilerParams(
            collective_id=0, has_side_effects=True, vmem_limit_bytes=60 * 1024 * 1024
        ),
    )(top_grad, stream, gain.astype(f32), weight, mask)
    return grads[None], wgrad[None]


def solution(mesh):
    placed = (
        P("section", None, "dp", None),
        P("section", None),
        P("section", None, None),
        P(),
        P(None, "dp", None),
    )
    return jax.shard_map(
        shards,
        mesh=mesh,
        in_specs=placed,
        out_specs=(P("section", None, "dp", None), P("section", "dp", None)),
        check_vma=False,
    )
```

time: 208 us -> 142 us (0.68)
  local copies, waits for them, and re-layouts: 35.1 us -> 5.36 us
  Pallas kernels: 112 us -> 133 us
  waiting for transfers between devices: 16.8 us -> 0 us
  between operations: 14.3 us -> 0.7 us
  matrix products: 11.5 us -> 0 us
  other arithmetic: 12.5 us -> 2.71 us
  starting transfers between devices: 5.22 us -> 0 us
    pallas_call x1, Pallas kernels: 112 us -> 133 us  [shards(): pl.pallas_call(functools.partial(relay, sections, ranks, micros, tokens),...]
    all_to_all x1 -> x0, waiting for transfers between devices: 16.8 us -> none  [shards(): lax.all_to_all(normed, 'dp', split_axis=2, concat_axis=1, tiled=True)]
    dot_general x3 -> x0, matrix products: 11.5 us -> none  [the longest x1 7.92 us: shards(): jnp.dot(normed.reshape(micros * tokens, model), weight, preferred_element...]
    unnamed x20 -> x4, local copies, waits for them, and re-layouts: 13.9 us -> 4.51 us
    convert_element_type x2 -> x0, local copies, waits for them, and re-layouts: 7.75 us -> none  [the longest x1 5.32 us: shards(): normed = (stream_f * inverse * gain_f[None]).astype(jnp.bfloat16)]
    all_to_all x1 -> x0, local copies, waits for them, and re-layouts: 5.26 us -> none  [shards(): lax.all_to_all(normed, 'dp', split_axis=2, concat_axis=1, tiled=True)]
    all_to_all x1 -> x0, starting transfers between devices: 5.18 us -> none  [shards(): lax.all_to_all(normed, 'dp', split_axis=2, concat_axis=1, tiled=True)]
    transpose x2 -> x0, other arithmetic: 4.05 us -> none  [the longest x1 2.73 us: shards(): jnp.transpose(normed.reshape(micros, tokens, KVH, GROUP, DH), (0, 2, 3, 1...]
  transfers between devices with their start and end apart: 2 -> 0, of which waited for: 1 -> 0; matrix products, arithmetic and copies ran while one was open for 16% -> 0% of each run, Pallas kernels for 0% -> 0%
where the time goes in v2:
time: 142 us
  Pallas kernels  133 us (94%)
  local copies, waits for them, and re-layouts  5.36 us (4%)
  other arithmetic  2.71 us (2%)
    pallas_call x1, Pallas kernels, shards(): pl.pallas_call(functools.partial(relay, sections, ranks, micros, tokens),...  133 us
    unnamed x4, local copies, waits for them, and re-layouts  4.51 us

profile of v2, /device:TPU:0, one launch (start us, length us, event | category | flops | bytes accessed | tf_op | source)
XLA Modules:
  0.0 141.6 jit_solution(14917881048665120022)
XLA Ops:
  0.7 1.0 compare_reduce_fusion.2
  1.7 0.1 iota_compare_fusion
  1.8 1.4 convert_element_type.10.gain
  3.2 0.1 broadcast_and_fusion.2
  3.3 0.1 and_convert_fusion
  3.4 0.8 copy.7.mask
  4.3 132.8 %shard_map.68 = (bf16[2,64,6144]{2,1,0:T(8,128)(2,1)}, bf16[1536,1024]{1,0:T(8,128)(2,1)}) custom-call(bf16[2,64,6144]{2,1,0:T(8,128)(2,1)} %top.1, bf16[2,64,6144]{2,1,0:T(8,128)(2,1)} %bitcast.7, f32[1,6144]{1,0:T(1,128)} %convert_element_type.10.gain, bf16[6144,1024]{1,0:T(8,128)(2,1)} %bitcast.5, f32[2,256,128]{2,1,0:T(8,128)} %copy.7.mask), custom_call_target="tpu_custom_call" | custom-call | tf_op jit(solution)/shard_map/pallas_call | solution.py:374
  137.1 0.0 copy-start
  137.1 2.8 %copy.10 = bf16[1,2,64,6144]{3,2,1,0:T(8,128)(2,1)} copy(bf16[1,2,64,6144]{3,2,1,0:T(8,128)(2,1)} %bitcast.8) | data formatting | bytes 3145728
  139.9 0.0 copy-done
  139.9 1.7 %copy.11 = bf16[1,1536,1024]{2,1,0:T(8,128)(2,1)} copy(bf16[1,1536,1024]{2,1,0:T(8,128)(2,1)S(1)} %bitcast.6) | data formatting | bytes 6291456
  (4 shorter events, 0.0 us)
Async XLA Ops:
  137.1 2.9 %copy-start = (bf16[1536,1024]{1,0:T(8,128)(2,1)S(1)}, bf16[1536,1024]{1,0:T(8,128)(2,1)}, u32[]{:S(2)}) copy-start(bf16[1536,1024]{1,0:T(8,128)(2,1)} %get-tuple-element.5) | copy-start | bytes 9437188

commit v3 on v2

--- a/solution.py
+++ b/solution.py
@@ -24,7 +24,7 @@
     top, stream, gain, weight_hbm, mask,
     grads, wgrad,
     weight, normed, inverse, keyval_own, keyval, keyval_raw, probs, attn, owned,
-    up, part, landed, dquery, total, dkv_all, mean,
+    up, part, landed, base, dkv_all, mean,
     weight_sem, keyval_send, keyval_recv, owned_send, owned_recv,
     up_send, up_recv, part_send, part_recv, dkv_send, dkv_recv,
 ):
@@ -36,14 +36,17 @@
     share = model // ranks
     f32, bf16 = jnp.float32, jnp.bfloat16
 
+    def span(low, size):
+        return pl.ds(low if isinstance(low, int) else pl.multiple_of(low, 128), size)
+
     def cols(g):
-        return pl.ds(pl.multiple_of(g * width, 128), width)
+        return span(g * width, width)
 
     def key_cols(g):
-        return pl.ds(pl.multiple_of(g * DH, DH), DH)
+        return span(g * DH, DH)
 
     def value_cols(g):
-        return pl.ds(pl.multiple_of((KVH + g) * DH, DH), DH)
+        return span((KVH + g) * DH, DH)
 
     def rank_rows(rank):
         return pl.ds(pl.multiple_of(rank * tokens, tokens), tokens)
@@ -56,12 +59,12 @@
             weight_hbm.at[cols(g), :], weight.at[cols(g), :], weight_sem.at[g]
         )
 
-    def keyval_copy(step):
+    def keyval_copy(m, step):
         return pltpu.make_async_remote_copy(
-            src_ref=keyval_own,
-            dst_ref=keyval.at[:, rank_rows(me), :],
-            send_sem=keyval_send.at[step - 1],
-            recv_sem=keyval_recv.at[step - 1],
+            src_ref=keyval_own.at[m],
+            dst_ref=keyval.at[m, rank_rows(me), :],
+            send_sem=keyval_send.at[m, step - 1],
+            recv_sem=keyval_recv.at[m, step - 1],
             device_id=(sec, lax.rem(me + step, ranks)),
             device_id_type=MESH,
         )
@@ -122,11 +125,12 @@
 
     keyval_own[...] = keyval_raw[...].astype(bf16)
     pl.semaphore_wait(barrier, 2 + ranks - 1)
-    for step in range(1, ranks):
-
-        @pl.when(me < ranks - step)
-        def _():
-            keyval_copy(step).start()
+    for m in range(micros):
+        for step in range(1, ranks):
+
+            @pl.when(me < ranks - step)
+            def _():
+                keyval_copy(m, step).start()
 
     for m in range(micros):
         keyval_raw[m] = keyval_raw[m] / inverse[m]
@@ -142,16 +146,22 @@
 
     for step in range(1, ranks):
 
-        @pl.when(me >= step)
-        def _():
-            keyval_copy(step).wait_recv()
-
-    @pl.when(sec < sections - 1)
+        @pl.when(me >= ranks - step)
+        def _():
+            landed[:, :, step - 1] = jnp.zeros((micros, KVH, tokens, 2 * DH), bf16)
+
+    @pl.when(sec < sections - 2)
     def _():
         for step in range(1, ranks):
             owned_copy(step).start()
 
     def forward(m, carry):
+        for step in range(1, ranks):
+
+            @pl.when(me >= step)
+            def _():
+                keyval_copy(m, step).wait_recv()
+
         @pl.loop(0, KVH)
         def _(g):
             queries = stacked(normed[m, :, cols(g)])
@@ -172,7 +182,9 @@
 
         return carry
 
-    lax.fori_loop(0, micros, forward, 0)
+    @pl.when(sec < sections - 1)
+    def _():
+        lax.fori_loop(0, micros, forward, 0)
 
     @pl.when(sec == sections - 1)
     def _():
@@ -241,41 +253,39 @@
 
         dq = lax.dot_general(dscores, keys, TN_DIMS, preferred_element_type=f32)
         dq = jnp.concatenate([dq[h * tokens : (h + 1) * tokens] for h in range(GROUP)], axis=1)
-        dquery[:, cols(g)] = dq
-        weighed = stream[m, :, cols(g)].astype(jnp.float32) * gain[:, cols(g)]
-        mean[...] += jnp.sum(weighed * dq, axis=-1, keepdims=True)
+        scaled = gain[:, cols(g)] * dq
+        mean[...] += jnp.sum(
+            stream[m, :, cols(g)].astype(f32) * scaled, axis=-1, keepdims=True
+        )
+        base[:, cols(g)] = up[m, :, cols(g)].astype(f32) + inverse[m] * scaled
 
     def gather(m, g):
-        total[...] = part[m, g, rank_rows(me), :].astype(jnp.float32)
         for step in range(1, ranks):
 
             @pl.when(me < ranks - step)
             def _():
                 part_copy(m, g, step - 1, lax.max(me - step, 0)).wait_recv()
-                total[...] += landed[m, g, step - 1].astype(jnp.float32)
-
-        rounded = total[...].astype(jnp.bfloat16)
+
+        terms = part[m, g, rank_rows(me), :].astype(f32)
+        for step in range(1, ranks):
+            terms = terms + landed[m, g, step - 1].astype(f32)
+        rounded = terms.astype(bf16)
         dkv_all[m, 0, :, key_cols(g)] = rounded[:, :DH]
         dkv_all[m, 0, :, value_cols(g)] = rounded[:, DH:]
         wide = rounded.astype(jnp.float32)
-        mean[...] += jnp.sum(
+        return (
             wide[:, :DH] * keyval_raw[m, :, key_cols(g)]
-            + wide[:, DH:] * keyval_raw[m, :, value_cols(g)],
-            axis=-1,
-            keepdims=True,
-        )
-
-    def project(m, g):
+            + wide[:, DH:] * keyval_raw[m, :, value_cols(g)]
+        )
+
+    def project(m, g, inv, pull):
         back = lax.dot_general(
             dkv_all[m, 0], weight[cols(g), :], NT_DIMS, preferred_element_type=jnp.float32
         )
-        scaled = gain[:, cols(g)] * (dquery[:, cols(g)] + back)
-        inv = inverse[m]
-        pull = inv * inv * inv * (mean[...] * (1.0 / model))
         fresh = (
-            up[m, :, cols(g)].astype(jnp.float32)
-            + inv * scaled
-            - stream[m, :, cols(g)].astype(jnp.float32) * pull
+            base[:, cols(g)]
+            + inv * (gain[:, cols(g)] * back)
+            - stream[m, :, cols(g)].astype(f32) * pull
         )
         grads[m, :, cols(g)] = fresh.astype(jnp.bfloat16)
 
@@ -284,17 +294,27 @@
             up_copy(m, g).start()
 
     def one_micro(m, carry):
+        @pl.when(sec == sections - 1)
+        def _():
+            forward(m, carry)
+
         mean[...] = jnp.zeros_like(mean)
         pl.loop(0, KVH)(functools.partial(attend, m))
-        pl.loop(0, KVH)(functools.partial(gather, m))
+        pulls = gather(m, 0)
+        for g in range(1, KVH):
+            pulls = pulls + gather(m, g)
         for step in range(ranks - 1):
             dkv_copy(m, step).start()
-        pl.loop(0, KVH)(functools.partial(project, m))
+        inv = inverse[m]
+        mean_all = mean[...] + jnp.sum(pulls, axis=-1, keepdims=True)
+        pull = inv * inv * inv * (mean_all * (1.0 / model))
+        for g in range(KVH):
+            project(m, g, inv, pull)
         return carry
 
     lax.fori_loop(0, micros, one_micro, 0)
 
-    @pl.when(sec == sections - 1)
+    @pl.when(sec >= sections - 2)
     def _():
         for step in range(1, ranks):
             owned_copy(step).start()
@@ -322,7 +342,8 @@
 
         @pl.when(me < ranks - step)
         def _():
-            keyval_copy(step).wait_send()
+            for m in range(micros):
+                keyval_copy(m, step).wait_send()
 
     for m in range(micros):
         for step in range(ranks - 1):
@@ -393,12 +414,11 @@
             pltpu.VMEM((micros, KVH, seq, 2 * DH), bf16),
             pltpu.VMEM((micros, KVH, ranks - 1, tokens, 2 * DH), bf16),
             pltpu.VMEM((tokens, model), f32),
-            pltpu.VMEM((tokens, 2 * DH), f32),
             pltpu.VMEM((micros, ranks, tokens, 2 * kv_width), bf16),
             pltpu.VMEM((tokens, 1), f32),
             pltpu.SemaphoreType.DMA((KVH,)),
-            pltpu.SemaphoreType.DMA((ranks - 1,)),
-            pltpu.SemaphoreType.DMA((ranks - 1,)),
+            pltpu.SemaphoreType.DMA((micros, ranks - 1)),
+            pltpu.SemaphoreType.DMA((micros, ranks - 1)),
             pltpu.SemaphoreType.DMA((ranks - 1,)),
             pltpu.SemaphoreType.DMA((ranks - 1,)),
             pltpu.SemaphoreType.DMA((micros, KVH)),

time: 142 us -> 131 us (0.923)
  Pallas kernels: 133 us -> 122 us
    pallas_call x1, Pallas kernels: 133 us -> 122 us  [shards(): pl.pallas_call(functools.partial(relay, sections, ranks, micros, tokens),...]
where the time goes in v3:
time: 131 us; the launch traced here: 130 us
  Pallas kernels  122 us (93%)
  local copies, waits for them, and re-layouts  5.36 us (4%)
  other arithmetic  2.71 us (2%)
    pallas_call x1, Pallas kernels, shards(): pl.pallas_call(functools.partial(relay, sections, ranks, micros, tokens),...  122 us
    unnamed x4, local copies, waits for them, and re-layouts  4.51 us

profile of v3, /device:TPU:0, one launch (start us, length us, event | category | flops | bytes accessed | tf_op | source)
XLA Modules:
  0.0 130.3 jit_solution(15167358759739313661)
XLA Ops:
  0.7 1.0 compare_reduce_fusion.2
  1.7 0.1 iota_compare_fusion
  1.8 1.4 %convert_element_type.10.gain = f32[1,6144]{1,0:T(1,128)} convert(bf16[1,6144]{1,0:T(2,128)(2,1)} %param.6) | non-fusion elementwise | flops 6144 | bytes 36864 | tf_op jit(solution)/shard_map/convert_element_type | solution.py:434
  3.2 0.1 broadcast_and_fusion.2
  3.3 0.1 and_convert_fusion
  3.4 0.8 copy.7.mask
  4.3 121.5 %shard_map.68 = (bf16[2,64,6144]{2,1,0:T(8,128)(2,1)}, bf16[1536,1024]{1,0:T(8,128)(2,1)}) custom-call(bf16[2,64,6144]{2,1,0:T(8,128)(2,1)} %top.1, bf16[2,64,6144]{2,1,0:T(8,128)(2,1)} %bitcast.7, f32[1,6144]{1,0:T(1,128)} %convert_element_type.10.gain, bf16[6144,1024]{1,0:T(8,128)(2,1)} %bitcast.5, f32[2,256,128]{2,1,0:T(8,128)} %copy.7.mask), custom_call_target="tpu_custom_call" | custom-call | tf_op jit(solution)/shard_map/pallas_call | solution.py:395
  125.8 0.0 copy-start
  125.8 2.8 %copy.10 = bf16[1,2,64,6144]{3,2,1,0:T(8,128)(2,1)} copy(bf16[1,2,64,6144]{3,2,1,0:T(8,128)(2,1)} %bitcast.8) | data formatting | bytes 3145728
  128.6 0.0 copy-done
  128.6 1.7 %copy.11 = bf16[1,1536,1024]{2,1,0:T(8,128)(2,1)} copy(bf16[1,1536,1024]{2,1,0:T(8,128)(2,1)S(1)} %bitcast.6) | data formatting | bytes 6291456
  (4 shorter events, 0.0 us)
Async XLA Ops:
  125.8 2.9 %copy-start = (bf16[1536,1024]{1,0:T(8,128)(2,1)S(1)}, bf16[1536,1024]{1,0:T(8,128)(2,1)}, u32[]{:S(2)}) copy-start(bf16[1536,1024]{1,0:T(8,128)(2,1)} %get-tuple-element.5) | copy-start | bytes 9437188

commit v4 on v3

--- a/solution.py
+++ b/solution.py
@@ -299,7 +299,8 @@
             forward(m, carry)
 
         mean[...] = jnp.zeros_like(mean)
-        pl.loop(0, KVH)(functools.partial(attend, m))
+        for g in range(KVH):
+            attend(m, g)
         pulls = gather(m, 0)
         for g in range(1, KVH):
             pulls = pulls + gather(m, g)

time: 131 us -> 131 us (level)
  no operation moved by 1% of the time
where the time goes in v4:
time: 131 us
  Pallas kernels  122 us (93%)
  local copies, waits for them, and re-layouts  5.36 us (4%)
  other arithmetic  2.71 us (2%)
    pallas_call x1, Pallas kernels, shards(): pl.pallas_call(functools.partial(relay, sections, ranks, micros, tokens),...  122 us
    unnamed x4, local copies, waits for them, and re-layouts  4.51 us

profile of v4, /device:TPU:0, one launch (start us, length us, event | category | flops | bytes accessed | tf_op | source)
XLA Modules:
  0.0 131.1 jit_solution(1634366258548344415)
XLA Ops:
  0.7 1.0 compare_reduce_fusion.2
  1.7 0.1 iota_compare_fusion
  1.8 1.4 %convert_element_type.10.gain = f32[1,6144]{1,0:T(1,128)} convert(bf16[1,6144]{1,0:T(2,128)(2,1)} %param.6) | non-fusion elementwise | flops 6144 | bytes 36864 | tf_op jit(solution)/shard_map/convert_element_type | solution.py:435
  3.2 0.1 broadcast_and_fusion.2
  3.3 0.1 and_convert_fusion
  3.4 0.8 copy.7.mask
  4.3 122.3 %shard_map.68 = (bf16[2,64,6144]{2,1,0:T(8,128)(2,1)}, bf16[1536,1024]{1,0:T(8,128)(2,1)}) custom-call(bf16[2,64,6144]{2,1,0:T(8,128)(2,1)} %top.1, bf16[2,64,6144]{2,1,0:T(8,128)(2,1)} %bitcast.7, f32[1,6144]{1,0:T(1,128)} %convert_element_type.10.gain, bf16[6144,1024]{1,0:T(8,128)(2,1)} %bitcast.5, f32[2,256,128]{2,1,0:T(8,128)} %copy.7.mask), custom_call_target="tpu_custom_call" | custom-call | tf_op jit(solution)/shard_map/pallas_call | solution.py:396
  126.6 0.0 copy-start
  126.6 2.8 %copy.10 = bf16[1,2,64,6144]{3,2,1,0:T(8,128)(2,1)} copy(bf16[1,2,64,6144]{3,2,1,0:T(8,128)(2,1)} %bitcast.8) | data formatting | bytes 3145728
  129.4 0.0 copy-done
  129.4 1.7 %copy.11 = bf16[1,1536,1024]{2,1,0:T(8,128)(2,1)} copy(bf16[1,1536,1024]{2,1,0:T(8,128)(2,1)S(1)} %bitcast.6) | data formatting | bytes 6291456
  (4 shorter events, 0.0 us)
Async XLA Ops:
  126.6 2.9 %copy-start = (bf16[1536,1024]{1,0:T(8,128)(2,1)S(1)}, bf16[1536,1024]{1,0:T(8,128)(2,1)}, u32[]{:S(2)}) copy-start(bf16[1536,1024]{1,0:T(8,128)(2,1)} %get-tuple-element.5) | copy-start | bytes 9437188
